TPU v7x, 128 devices: a whole 4x4x4 slice. The times are simulated.
128 devices in a mesh: seq: 32 (over x, y, core), head: 4 (over z).
Axes of the slice: x: 4, y: 4, z: 4, core: 2. Of those that a mesh axis runs over, the one named last changes fastest.
Arguments:
- queries: bfloat16 [8192, 2048], P('seq', 'head'), may hold values from -6 to 6
- keys: bfloat16 [8192, 2048], P('seq', 'head'), may hold values from -4 to 4
- values: bfloat16 [8192, 2048], P('seq', 'head'), may hold values from -4 to 4
- rates: float32 [8192, 32], P('seq', 'head'), may hold values from 0 to 0.004938272
- start_state: float32 [32, 64, 65], P('head'), may hold values from -2 to 2
- out_weight: bfloat16 [2048, 2048], P('head'), may hold values from -0.125 to 0.125
Outputs:
- mixed: bfloat16 [8192, 2048], P(('seq', 'head'))
All inputs are finite; a program needn't handle non-finite values.
Results may differ from a plain program's by a relative error of at most 0.015.
Values may be sent and summed in bfloat16 or wider, within the bound.
A program may use at most 192 MiB of HBM per device.

v0:
```python
import jax
import jax.numpy as jnp
from jax import lax
from jax.experimental import pallas as pl
from jax.experimental.pallas import tpu as pltpu
from jax.sharding import PartitionSpec as P

HD = 64
MINIBATCH_TOKENS = 16
TOK = 256
HALF = TOK // 2
PAIRS = 4
GROUP = 8
GROUPS = 4
RING = 4
FEAT = 80
LANES = 128
WIDTH = 2048
ROWS = TOK // RING
MESH = pl.DeviceIdType.MESH
F32 = jnp.float32
BF16 = jnp.bfloat16


def dot(left, right):
    return jnp.dot(left, right, preferred_element_type=F32)


def kernel(
    q_hbm, k_hbm, v_hbm, rate_ref, start_hbm, w_hbm, out_ref,
    q_ref, k_ref, v_ref, w_ref, start_ref,
    u_ref, kt_ref, qt_ref, py_ref,
    send1, recv1, prefix, send2, recv2, state, send3, recv3,
    far_send, far_recv, near_send, near_recv,
    load_sem, send_sem1, recv_sem1, send_sem2, recv_sem2, send_sem3, recv_sem3,
    far_send_sem, far_recv_sem, near_send_sem, near_recv_sem,
):
    seq = lax.axis_index("seq")
    head = lax.axis_index("head")
    group = seq // GROUP
    place = lax.rem(seq, GROUP)
    chip = place // 2
    core = lax.rem(place, 2)
    base = group * GROUP

    loads = [
        pltpu.make_async_copy(k_hbm, k_ref, load_sem.at[0]),
        pltpu.make_async_copy(v_hbm, v_ref, load_sem.at[1]),
        pltpu.make_async_copy(q_hbm, q_ref, load_sem.at[2]),
        pltpu.make_async_copy(start_hbm.at[place], start_ref, load_sem.at[3]),
        pltpu.make_async_copy(w_hbm, w_ref, load_sem.at[4]),
    ]
    for load in loads:
        load.start()

    recv3[:, FEAT:, :] = jnp.zeros((GROUP, LANES - FEAT, LANES), BF16)

    barrier = pltpu.get_barrier_semaphore()
    for step in range(1, GROUP):
        pl.semaphore_signal(
            barrier, inc=1, device_id=(base + lax.rem(place + step, GROUP), head), device_id_type=MESH
        )
    for step in range(1, GROUPS):
        pl.semaphore_signal(
            barrier, inc=1,
            device_id=(lax.rem(group + step, GROUPS) * GROUP + place, head), device_id_type=MESH,
        )
    up = lax.rem(head + 1, RING)
    down = lax.rem(head + RING - 1, RING)
    for peer in (up, down):
        pl.semaphore_signal(barrier, inc=1, device_id=(seq, peer), device_id_type=MESH)

    lane = lax.broadcasted_iota(jnp.int32, (TOK, LANES), 1)
    is_one = jnp.where(lane == HD, 1.0, 0.0).astype(F32)
    row_h = lax.broadcasted_iota(jnp.int32, (HALF, HALF), 0)
    col_h = lax.broadcasted_iota(jnp.int32, (HALF, HALF), 1)
    earlier_block = row_h // MINIBATCH_TOKENS > col_h // MINIBATCH_TOKENS
    same_chunk = row_h // HD == col_h // HD
    near_mask = jnp.logical_and(earlier_block, same_chunk)
    far_mask = jnp.logical_and(earlier_block, jnp.logical_not(same_chunk))
    causal = row_h >= col_h

    def with_one(pair, odd):
        wide = pair.astype(F32)
        if odd:
            wide = pltpu.roll(wide, HD, 1)
        return jnp.where(lane < HD, wide, is_one)

    def build_maps(slot, p):
        cols = pl.ds(pl.multiple_of(p * LANES, LANES), LANES)
        kp = k_ref[:, cols]
        vp = v_ref[:, cols]
        two = (0, 1)
        kf = [with_one(kp, e) for e in two]
        kx = [kf[e].astype(BF16) for e in two]
        ktf = [jnp.transpose(kf[e]) for e in two]
        kt = [ktf[e].astype(BF16) for e in two]
        rate = [rate_ref[pl.ds(2 * p + e, 1), :] for e in two]
        vx = [jnp.where((lane < HD) == (e == 0), vp.astype(F32), 0.0).astype(BF16) for e in two]
        x = [jnp.concatenate([kx[e], vx[e]], axis=1) for e in two]
        low = [dot(kx[e], kt[e]) * rate[e] for e in two]
        lows = [(low[e][:HALF, :HALF], low[e][HALF:, HALF:]) for e in two]
        cross = [low[e][HALF:, :HALF].astype(BF16) for e in two]
        both = [(e, b) for e in two for b in two]
        near = {eb: jnp.where(near_mask, lows[eb[0]][eb[1]], 0.0) for eb in both}
        far = {eb: jnp.where(far_mask, lows[eb[0]][eb[1]], 0.0) for eb in both}
        near_b = {eb: near[eb].astype(BF16) for eb in both}
        sq = {eb: dot(near_b[eb], near_b[eb]) for eb in both}
        n64 = {eb: sq[eb] - near[eb] - dot(near_b[eb], sq[eb].astype(BF16)) for eb in both}
        n64_b = {eb: n64[eb].astype(BF16) for eb in both}
        z = {eb: far[eb] + dot(n64_b[eb], far[eb].astype(BF16)) for eb in both}
        inv = {
            eb: (n64[eb] - z[eb] - dot(z[eb].astype(BF16), n64_b[eb])).astype(BF16) for eb in both
        }
        x0 = [x[e][:HALF] for e in two]
        u0 = [(x0[e].astype(F32) + dot(inv[e, 0], x0[e])).astype(BF16) for e in two]
        x1 = [x[e][HALF:].astype(F32) - dot(cross[e], u0[e]) for e in two]
        u1 = [(x1[e] + dot(inv[e, 1], x1[e].astype(BF16))).astype(BF16) for e in two]
        sign = jnp.where(
            lax.broadcasted_iota(jnp.int32, (FEAT, 2 * LANES), 1) < LANES, -1.0, 1.0
        ).astype(F32)
        for e in two:
            u = jnp.concatenate([u0[e], u1[e]], axis=0)
            u_ref[2 * p + e] = u
            kt_ref[2 * p + e] = kt[e]
            krt = (ktf[e][:FEAT] * rate[e]).astype(BF16)
            send1[slot, e] = (dot(krt, u) * sign).astype(BF16)

    def build_outputs(p):
        qp = q_ref[:, p * LANES : (p + 1) * LANES]
        total = None
        for e in (0, 1):
            qf = with_one(qp, e)
            scores = dot(qf.astype(BF16), kt_ref[2 * p + e]) * rate_ref[2 * p + e : 2 * p + e + 1, :]
            top = jnp.where(causal, scores[:HALF, :HALF], 0.0).astype(BF16)
            last = jnp.where(causal, scores[HALF:, HALF:], 0.0).astype(BF16)
            bottom = jnp.concatenate([scores[HALF:, :HALF].astype(BF16), last], axis=1)
            pu = jnp.concatenate(
                [dot(top, u_ref[2 * p + e, :HALF, :]), dot(bottom, u_ref[2 * p + e])], axis=0
            )
            qt_ref[p, :, e * LANES : (e + 1) * LANES] = (qf - pu[:, :LANES]).astype(BF16)
            total = pu[:, LANES:] if total is None else total + pu[:, LANES:]
        py_ref[p] = total

    def to_group(slot, e, peer):
        return pltpu.make_async_remote_copy(
            src_ref=send1.at[slot, e],
            dst_ref=recv1.at[place],
            send_sem=send_sem1.at[slot, e],
            recv_sem=recv_sem1.at[place],
            device_id=(base + peer, head),
            device_id_type=MESH,
        )

    copies = []
    loads[0].wait()
    loads[1].wait()
    for slot, step in enumerate((2, 1, 3, 0)):
        p = lax.rem(chip + step, PAIRS)
        build_maps(slot, p)
        if slot == 0:
            pl.semaphore_wait(barrier, GROUP - 1 + GROUPS - 1 + 2)
        if step:
            for e in (0, 1):
                copy = to_group(slot, e, 2 * p + e)
                copy.start()
                copies.append(copy)
        else:
            copy = to_group(slot, 1 - core, 2 * p + 1 - core)
            copy.start()
            copies.append(copy)
            recv1[place] = send1[slot, core]

    loads[2].wait()
    build_outputs(0)
    build_outputs(1)

    pad = jnp.zeros((LANES - FEAT, 2 * LANES), BF16)
    total = None
    for j in range(GROUP):
        @pl.when(place != j)
        def _(j=j):
            pltpu.make_async_remote_copy(
                src_ref=send1.at[0, 0],
                dst_ref=recv1.at[j],
                send_sem=send_sem1.at[0, 0],
                recv_sem=recv_sem1.at[j],
                device_id=(base + j, head),
                device_id_type=MESH,
            ).wait_recv()

        here = recv1[j]
        if total is None:
            total = here.astype(F32)
        else:
            rounded = total.astype(BF16)
            prefix[j - 1] = rounded
            total = total + here.astype(F32) + dot(
                here[:, :LANES], jnp.concatenate([rounded, pad], axis=0)
            )
    send2[...] = total.astype(BF16)

    def to_groups(step):
        return pltpu.make_async_remote_copy(
            src_ref=send2,
            dst_ref=recv2.at[group],
            send_sem=send_sem2.at[step - 1],
            recv_sem=recv_sem2.at[group],
            device_id=((group + step) * GROUP + place, head),
            device_id_type=MESH,
        )

    for step in range(1, GROUPS):
        @pl.when(group + step < GROUPS)
        def _(step=step):
            to_groups(step).start()

    build_outputs(2)

    loads[3].wait()
    first = jnp.concatenate([start_ref[...], jnp.zeros((HD, LANES - HD - 1), F32)], axis=1)
    nothing = jnp.zeros((HD, LANES), F32)
    stacked = jnp.concatenate(
        [jnp.where(core == 0, first, nothing), jnp.where(core == 1, first, nothing)], axis=0
    )
    state[...] = jnp.transpose(stacked)
    for g in range(GROUPS - 1):
        @pl.when(g < group)
        def _(g=g):
            pltpu.make_async_remote_copy(
                src_ref=send2,
                dst_ref=recv2.at[g],
                send_sem=send_sem2.at[0],
                recv_sem=recv_sem2.at[g],
                device_id=(g * GROUP + place, head),
                device_id_type=MESH,
            ).wait_recv()
            step_map = recv2[g]
            old = state[...]
            state[:FEAT, :] = (
                old[:FEAT]
                + step_map[:, LANES:].astype(F32)
                + dot(step_map[:, :LANES], old.astype(BF16))
            )

    entry = state[...]
    entry_b = entry.astype(BF16)
    send3[0] = entry_b[:FEAT]
    for j in range(1, GROUP):
        before = prefix[j - 1]
        send3[j] = (
            entry[:FEAT] + before[:, LANES:].astype(F32) + dot(before[:, :LANES], entry_b)
        ).astype(BF16)

    def back(step):
        peer = lax.rem(place + step, GROUP)
        return pltpu.make_async_remote_copy(
            src_ref=send3.at[peer],
            dst_ref=recv3.at[place, pl.ds(0, FEAT)],
            send_sem=send_sem3.at[step - 1],
            recv_sem=recv_sem3.at[place],
            device_id=(base + peer, head),
            device_id_type=MESH,
        )

    for step in (4, 5, 3, 2, 6, 7, 1):
        copy = back(step)
        copy.start()
        copies.append(copy)
    recv3[place, :FEAT, :] = send3[place]

    build_outputs(3)

    for step in range(1, GROUP):
        source = lax.rem(place + step, GROUP)
        pltpu.make_async_remote_copy(
            src_ref=send3.at[0],
            dst_ref=recv3.at[source, pl.ds(0, FEAT)],
            send_sem=send_sem3.at[0],
            recv_sem=recv_sem3.at[source],
            device_id=(base + source, head),
            device_id_type=MESH,
        ).wait_recv()
    loads[4].wait()

    states = [
        jnp.concatenate([recv3[2 * p], recv3[2 * p + 1]], axis=0) for p in range(PAIRS)
    ]

    def outputs_of(block):
        rows = pl.ds(pl.multiple_of(block * ROWS, ROWS), ROWS)
        return jnp.concatenate(
            [
                (dot(qt_ref[p, rows, :], states[p]) + py_ref[p, rows, :]).astype(BF16)
                for p in range(PAIRS)
            ],
            axis=1,
        )

    half = WIDTH // 2

    def project(z, side, piece):
        at = side * half + piece * 512
        return dot(z, w_ref[:, at : at + 512])

    def send(source, target, send_at, recv_at, peer):
        copy = pltpu.make_async_remote_copy(
            src_ref=source, dst_ref=target, send_sem=send_at, recv_sem=recv_at,
            device_id=(seq, peer), device_id_type=MESH,
        )
        copy.start()
        copies.append(copy)

    def arrived(target, recv_at, peer):
        pltpu.make_async_remote_copy(
            src_ref=far_send.at[0], dst_ref=target, send_sem=far_send_sem.at[0], recv_sem=recv_at,
            device_id=(seq, peer), device_id_type=MESH,
        ).wait_recv()

    z = outputs_of(lax.rem(head + 2, RING))
    for side, peer in ((0, up), (1, down)):
        for piece in (0, 1):
            far_send[side, :, piece * 512 : (piece + 1) * 512] = project(z, side, piece).astype(BF16)
        send(far_send.at[side], far_recv.at[side], far_send_sem.at[side], far_recv_sem.at[side], peer)
    z_near = [outputs_of(up), outputs_of(down)]
    for way, peer in ((0, up), (1, down)):
        side = 1 - way
        for piece in (0, 1):
            near_send[way, side, :, piece * 512 : (piece + 1) * 512] = project(
                z_near[way], side, piece
            ).astype(BF16)
        send(
            near_send.at[way, side], near_recv.at[way, side],
            near_send_sem.at[way, side], near_recv_sem.at[way, side], peer,
        )
    for way, peer, source in ((0, up, down), (1, down, up)):
        side = way
        arrived(far_recv.at[side], far_recv_sem.at[side], source)
        for piece in (0, 1):
            cols = slice(piece * 512, (piece + 1) * 512)
            near_send[way, side, :, cols] = (
                project(z_near[way], side, piece) + far_recv[side, :, cols].astype(F32)
            ).astype(BF16)
        send(
            near_send.at[way, side], near_recv.at[way, side],
            near_send_sem.at[way, side], near_recv_sem.at[way, side], peer,
        )
    z = outputs_of(head)
    own = [[project(z, side, piece) for piece in (0, 1)] for side in (0, 1)]
    for way, side in ((0, 1), (1, 0), (0, 0), (1, 1)):
        arrived(near_recv.at[way, side], near_recv_sem.at[way, side], down if way == 0 else up)
    for side in (0, 1):
        for piece in (0, 1):
            cols = slice(piece * 512, (piece + 1) * 512)
            at = side * half + piece * 512
            out_ref[:, at : at + 512] = (
                own[side][piece]
                + near_recv[0, side, :, cols].astype(F32)
                + near_recv[1, side, :, cols].astype(F32)
            ).astype(BF16)

    for copy in copies:
        copy.wait_send()
    for step in range(1, GROUPS):
        @pl.when(group + step < GROUPS)
        def _(step=step):
            to_groups(step).wait_send()


def per_device(queries, keys, values, rates, start_state, out_weight):
    hbm = pl.BlockSpec(memory_space=pl.ANY)
    vmem = pl.BlockSpec(memory_space=pltpu.VMEM)
    dma = pltpu.SemaphoreType.DMA
    half = WIDTH // 2
    return pl.pallas_call(
        kernel,
        out_shape=jax.ShapeDtypeStruct((ROWS, WIDTH), BF16),
        in_specs=[hbm, hbm, hbm, vmem, hbm, hbm],
        out_specs=vmem,
        scratch_shapes=[
            pltpu.VMEM((TOK, 8 * HD), BF16),
            pltpu.VMEM((TOK, 8 * HD), BF16),
            pltpu.VMEM((TOK, 8 * HD), BF16),
            pltpu.VMEM((8 * HD, WIDTH), BF16),
            pltpu.VMEM((HD, HD + 1), F32),
            pltpu.VMEM((2 * PAIRS, TOK, 2 * LANES), BF16),
            pltpu.VMEM((2 * PAIRS, LANES, TOK), BF16),
            pltpu.VMEM((PAIRS, TOK, 2 * LANES), BF16),
            pltpu.VMEM((PAIRS, TOK, LANES), F32),
            pltpu.VMEM((PAIRS, 2, FEAT, 2 * LANES), BF16),
            pltpu.VMEM((GROUP, FEAT, 2 * LANES), BF16),
            pltpu.VMEM((GROUP - 1, FEAT, 2 * LANES), BF16),
            pltpu.VMEM((FEAT, 2 * LANES), BF16),
            pltpu.VMEM((GROUPS, FEAT, 2 * LANES), BF16),
            pltpu.VMEM((LANES, LANES), F32),
            pltpu.VMEM((GROUP, FEAT, LANES), BF16),
            pltpu.VMEM((GROUP, LANES, LANES), BF16),
            pltpu.VMEM((2, ROWS, half), BF16),
            pltpu.VMEM((2, ROWS, half), BF16),
            pltpu.VMEM((2, 2, ROWS, half), BF16),
            pltpu.VMEM((2, 2, ROWS, half), BF16),
            dma((5,)),
            dma((PAIRS, 2)),
            dma((GROUP,)),
            dma((GROUPS - 1,)),
            dma((GROUPS,)),
            dma((GROUP - 1,)),
            dma((GROUP,)),
            dma((2,)),
            dma((2,)),
            dma((2, 2)),
            dma((2, 2)),
        ],
        compiler_params=pltpu.CompilerParams(
            collective_id=0, has_side_effects=True, vmem_limit_bytes=48 * 1024 * 1024
        ),
    )(queries, keys, values, jnp.transpose(rates), start_state, out_weight)


def solution(mesh):
    in_specs = (
        P("seq", "head"),
        P("seq", "head"),
        P("seq", "head"),
        P("seq", "head"),
        P("head", None, None),
        P("head", None),
    )
    out_specs = P(("seq", "head"), None)
    return jax.shard_map(
        per_device, mesh=mesh, in_specs=in_specs, out_specs=out_specs, check_vma=False
    )
```

profile of v0, /device:TPU:6, one launch (start us, length us, event | category | flops | bytes accessed | tf_op | source)
XLA Modules:
  0.0 40.4 jit_solution(8387993034340377395)
XLA Ops:
  0.0 0.0 copy-start
  0.0 1.6 %copy-done = bf16[512,2048]{1,0:T(8,128)(2,1)S(1)} copy-done((bf16[512,2048]{1,0:T(8,128)(2,1)S(1)}, bf16[512,2048]{1,0:T(8,128)(2,1)}, u32[]{:S(2)}) %copy-start) | copy-done | bytes 2097176
  1.6 0.0 copy-start.1
  1.6 0.9 %copy-done.1 = bf16[256,512]{1,0:T(8,128)(2,1)S(1)} copy-done((bf16[256,512]{1,0:T(8,128)(2,1)S(1)}, bf16[256,512]{1,0:T(8,128)(2,1)}, u32[]{:S(2)}) %copy-start.1) | copy-done | bytes 262168
  2.5 0.0 copy-start.2
  2.5 0.9 %copy-done.2 = bf16[256,512]{1,0:T(8,128)(2,1)S(1)} copy-done((bf16[256,512]{1,0:T(8,128)(2,1)S(1)}, bf16[256,512]{1,0:T(8,128)(2,1)}, u32[]{:S(2)}) %copy-start.2) | copy-done | bytes 262168
  3.5 0.0 copy-start.3
  3.5 0.9 %copy-done.3 = bf16[256,512]{1,0:T(8,128)(2,1)S(1)} copy-done((bf16[256,512]{1,0:T(8,128)(2,1)S(1)}, bf16[256,512]{1,0:T(8,128)(2,1)}, u32[]{:S(2)}) %copy-start.3) | copy-done | bytes 262168
  4.4 0.0 copy-start.4
  4.4 0.9 %copy-done.4 = f32[8,64,65]{2,1,0:T(8,128)S(1)} copy-done((f32[8,64,65]{2,1,0:T(8,128)S(1)}, f32[8,64,65]{2,1,0:T(8,128)}, u32[]{:S(2)}) %copy-start.4) | copy-done | bytes 133144
  5.4 0.0 copy-start.5
  5.4 0.7 %copy-done.5 = f32[256,8]{0,1:T(8,128)S(1)} copy-done((f32[256,8]{0,1:T(8,128)S(1)}, f32[256,8]{0,1:T(8,128)}, u32[]{:S(2)}) %copy-start.5) | copy-done | bytes 8216
  6.1 33.6 %shard_map.64 = bf16[64,2048]{1,0:T(8,128)(2,1)S(1)} custom-call(bf16[256,512]{1,0:T(8,128)(2,1)S(1)} %copy-done.1, bf16[256,512]{1,0:T(8,128)(2,1)S(1)} %copy-done.2, bf16[256,512]{1,0:T(8,128)(2,1)S(1)} %copy-done.3, f32[8,256]{1,0:T(8,128)S(1)} %bitcast.1, f32[8,64,65]{2,1,0:T(8,128)S(1)} %copy-done.4, bf16[512,2048]{1,0:T(8,128)(2,1)S(1)} %copy-done), custom_call_target="tpu_custom_call" | custom-call | tf_op jit(solution)/shard_map/pallas_call | solution.py:375
  39.7 0.7 %copy.8 = bf16[64,2048]{1,0:T(8,128)(2,1)} copy(bf16[64,2048]{1,0:T(8,128)(2,1)S(1)} %shard_map.64) | data formatting | bytes 524288
Async XLA Ops:
  0.0 1.6 %copy-start = (bf16[512,2048]{1,0:T(8,128)(2,1)S(1)}, bf16[512,2048]{1,0:T(8,128)(2,1)}, u32[]{:S(2)}) copy-start(bf16[512,2048]{1,0:T(8,128)(2,1)} %w_hbm.1) | copy-start | bytes 6291460
  1.6 0.9 %copy-start.1 = (bf16[256,512]{1,0:T(8,128)(2,1)S(1)}, bf16[256,512]{1,0:T(8,128)(2,1)}, u32[]{:S(2)}) copy-start(bf16[256,512]{1,0:T(8,128)(2,1)} %q_hbm.1) | copy-start | bytes 786436
  2.5 0.9 %copy-start.2 = (bf16[256,512]{1,0:T(8,128)(2,1)S(1)}, bf16[256,512]{1,0:T(8,128)(2,1)}, u32[]{:S(2)}) copy-start(bf16[256,512]{1,0:T(8,128)(2,1)} %k_hbm.1) | copy-start | bytes 786436
  3.5 0.9 %copy-start.3 = (bf16[256,512]{1,0:T(8,128)(2,1)S(1)}, bf16[256,512]{1,0:T(8,128)(2,1)}, u32[]{:S(2)}) copy-start(bf16[256,512]{1,0:T(8,128)(2,1)} %v_hbm.1) | copy-start | bytes 786436
  4.4 0.9 %copy-start.4 = (f32[8,64,65]{2,1,0:T(8,128)S(1)}, f32[8,64,65]{2,1,0:T(8,128)}, u32[]{:S(2)}) copy-start(f32[8,64,65]{2,1,0:T(8,128)} %start_hbm.1) | copy-start | bytes 399364
  5.4 0.7 %copy-start.5 = (f32[256,8]{0,1:T(8,128)S(1)}, f32[256,8]{0,1:T(8,128)}, u32[]{:S(2)}) copy-start(f32[256,8]{0,1:T(8,128)} %param.9) | copy-start | bytes 24580
where the time goes:
time: 40.7 us; the launch traced here: 40.4 us
  Pallas kernels  33.6 us (83%)
  local copies, waits for them, and re-layouts  6.79 us (17%)
    pallas_call x1, Pallas kernels, per_device(): pl.pallas_call(kernel, out_shape=jax.ShapeDtypeStruct((ROWS, WIDTH), BF16...  33.6 us
    unnamed x13, local copies, waits for them, and re-layouts  6.79 us

commit v1 on v0

v1 whole, which is shorter than its diff:
```python
import jax
import jax.numpy as jnp
from jax import lax
from jax.experimental import pallas as pl
from jax.experimental.pallas import tpu as pltpu
from jax.sharding import PartitionSpec as P

HD = 64
MINIBATCH_TOKENS = 16
TOK = 256
HALF = TOK // 2
PAIRS = 4
GROUP = 8
GROUPS = 4
RING = 4
FEAT = 80
LANES = 128
PACKED = 48
WIDTH = 2048
ROWS = TOK // RING
CHUNKS = 4
CHUNK = ROWS // CHUNKS
MESH = pl.DeviceIdType.MESH
F32 = jnp.float32
BF16 = jnp.bfloat16


def dot(left, right):
    return jnp.dot(left, right, preferred_element_type=F32)


def dot_t(left, right):
    return lax.dot_general(left, right, (((1,), (1,)), ((), ())), preferred_element_type=F32)


def kernel(
    q_hbm, k_hbm, v_hbm, rate_hbm, start_hbm, w_hbm, out_ref,
    q_ref, k_ref, v_ref, w_ref, start_ref, rate_ref,
    u_ref, kt_ref, qt_ref, py_ref,
    send1, recv1, prefix, send2, recv2, send3, recv3,
    far_send, far_recv, near_send, near_recv,
    load_sem, send_sem1, recv_sem1, send_sem2, recv_sem2, send_sem3, recv_sem3,
    far_send_sem, far_recv_sem, near_send_sem, near_recv_sem, merge_send_sem, merge_recv_sem,
):
    seq = lax.axis_index("seq")
    head = lax.axis_index("head")
    group = seq // GROUP
    place = lax.rem(seq, GROUP)
    chip = place // 2
    core = lax.rem(place, 2)
    base = group * GROUP

    loads = [
        pltpu.make_async_copy(k_hbm, k_ref, load_sem.at[0]),
        pltpu.make_async_copy(v_hbm, v_ref, load_sem.at[1]),
        pltpu.make_async_copy(q_hbm, q_ref, load_sem.at[2]),
        pltpu.make_async_copy(start_hbm.at[place], start_ref, load_sem.at[3]),
        pltpu.make_async_copy(w_hbm, w_ref, load_sem.at[4]),
        pltpu.make_async_copy(rate_hbm, rate_ref, load_sem.at[5]),
    ]
    for load in (loads[5], loads[0], loads[1]):
        load.start()

    barrier = pltpu.get_barrier_semaphore()
    for step in range(1, GROUP):
        pl.semaphore_signal(
            barrier, inc=1, device_id=(base + lax.rem(place + step, GROUP), head), device_id_type=MESH
        )
    for step in range(1, GROUPS):
        pl.semaphore_signal(
            barrier, inc=1,
            device_id=(lax.rem(group + step, GROUPS) * GROUP + place, head), device_id_type=MESH,
        )
    up = lax.rem(head + 1, RING)
    down = lax.rem(head + RING - 1, RING)
    for peer in (up, down):
        pl.semaphore_signal(barrier, inc=1, device_id=(seq, peer), device_id_type=MESH)

    lane = lax.broadcasted_iota(jnp.int32, (TOK, LANES), 1)
    is_one = jnp.where(lane == HD, 1.0, 0.0).astype(F32)
    row_h = lax.broadcasted_iota(jnp.int32, (HALF, HALF), 0)
    col_h = lax.broadcasted_iota(jnp.int32, (HALF, HALF), 1)
    earlier_block = row_h // MINIBATCH_TOKENS > col_h // MINIBATCH_TOKENS
    same_chunk = row_h // HD == col_h // HD
    near_mask = jnp.logical_and(earlier_block, same_chunk)
    far_mask = jnp.logical_and(earlier_block, jnp.logical_not(same_chunk))
    causal = row_h >= col_h

    one_b = is_one.astype(BF16)
    lane_f = lane[:FEAT]
    row_f = lax.broadcasted_iota(jnp.int32, (FEAT, LANES), 0)
    sign = jnp.where(lane_f < HD, -1.0, 1.0).astype(F32)
    lane_t = lane[:16]
    row_t = lax.broadcasted_iota(jnp.int32, (16, LANES), 0)
    pick = jnp.where(jnp.logical_and(row_t == 1, lane_t == HD), 1.0, 0.0).astype(BF16)
    diagonal = jnp.where(row_f == lane_f, 1.0, 0.0).astype(BF16)
    rest = jnp.zeros((LANES - FEAT, LANES), BF16)

    def pack(wide, column):
        in_row = dot_t(pick, jnp.concatenate([column.astype(BF16), rest], axis=0))
        return jnp.concatenate([wide[:HD], wide[HD:] + in_row], axis=0).astype(BF16)

    def unpack(packed):
        wide = packed.astype(F32)
        in_row = jnp.where(row_t == 0, pltpu.roll(wide[HD:], 15, 0), 0.0).astype(BF16)
        column = dot_t(
            diagonal, jnp.concatenate([jnp.zeros((HD, LANES), BF16), in_row, rest], axis=0)
        )
        wide = jnp.where(row_f <= HD, wide, 0.0)
        return (
            jnp.where(lane_f < HD, wide, column).astype(BF16),
            jnp.concatenate([wide, column], axis=1),
        )

    def with_one(pair, odd):
        wide = pair.astype(F32)
        if odd:
            wide = pltpu.roll(wide, HD, 1)
        return jnp.where(lane < HD, wide, is_one)

    def build_maps(slots, pairs):
        heads = [(i, e) for i in range(len(pairs)) for e in (0, 1)]
        at = {h: 2 * pairs[h[0]] + h[1] for h in heads}
        cols = [pl.ds(pl.multiple_of(p * LANES, LANES), LANES) for p in pairs]
        kp = [k_ref[:, c] for c in cols]
        vp = [v_ref[:, c].astype(F32) for c in cols]
        vf = {h: vp[h[0]] if h[1] else pltpu.roll(vp[h[0]], HD, 1) for h in heads}
        kf = {h: with_one(kp[h[0]], h[1]) for h in heads}
        kx = {h: kf[h].astype(BF16) for h in heads}
        ktf = {h: jnp.transpose(kf[h]) for h in heads}
        kt = {h: ktf[h].astype(BF16) for h in heads}
        rate = {h: rate_ref[pl.ds(at[h], 1), :] for h in heads}
        x = {
            h: jnp.concatenate([jnp.where(lane < HD, kf[h], vf[h]).astype(BF16), one_b], axis=1)
            for h in heads
        }
        low = {h: dot(kx[h], kt[h]) * rate[h] for h in heads}
        lows = {h: (low[h][:HALF, :HALF], low[h][HALF:, HALF:]) for h in heads}
        cross = {h: low[h][HALF:, :HALF].astype(BF16) for h in heads}
        both = [(h, b) for h in heads for b in (0, 1)]
        near = {hb: jnp.where(near_mask, lows[hb[0]][hb[1]], 0.0) for hb in both}
        far = {hb: jnp.where(far_mask, lows[hb[0]][hb[1]], 0.0) for hb in both}
        near_b = {hb: near[hb].astype(BF16) for hb in both}
        sq = {hb: dot(near_b[hb], near_b[hb]) for hb in both}
        n64 = {hb: sq[hb] - near[hb] - dot(near_b[hb], sq[hb].astype(BF16)) for hb in both}
        n64_b = {hb: n64[hb].astype(BF16) for hb in both}
        z = {hb: far[hb] + dot(n64_b[hb], far[hb].astype(BF16)) for hb in both}
        inv = {
            hb: (n64[hb] - z[hb] - dot(z[hb].astype(BF16), n64_b[hb])).astype(BF16) for hb in both
        }
        x0 = {h: x[h][:HALF] for h in heads}
        u0 = {h: (x0[h].astype(F32) + dot(inv[h, 0], x0[h])).astype(BF16) for h in heads}
        x1 = {h: x[h][HALF:].astype(F32) - dot(cross[h], u0[h]) for h in heads}
        u1 = {h: (x1[h] + dot(inv[h, 1], x1[h].astype(BF16))).astype(BF16) for h in heads}
        u = {h: jnp.concatenate([u0[h], u1[h]], axis=0) for h in heads}
        krt = {h: (ktf[h][:FEAT] * rate[h]).astype(BF16) for h in heads}
        maps = {h: dot(krt[h], u[h]) for h in heads}
        for h in heads:
            send1[slots[h[0]], h[1]] = pack(maps[h][:, :LANES] * sign, -maps[h][:, LANES:])
        for h in heads:
            u_ref[at[h]] = u[h]
            kt_ref[at[h]] = kt[h]

    def build_outputs(p):
        qp = q_ref[:, p * LANES : (p + 1) * LANES]
        for e in (0, 1):
            qf = with_one(qp, e)
            scores = dot(qf.astype(BF16), kt_ref[2 * p + e]) * rate_ref[2 * p + e : 2 * p + e + 1, :]
            top = jnp.where(causal, scores[:HALF, :HALF], 0.0).astype(BF16)
            last = jnp.where(causal, scores[HALF:, HALF:], 0.0).astype(BF16)
            bottom = jnp.concatenate([scores[HALF:, :HALF].astype(BF16), last], axis=1)
            pu = jnp.concatenate(
                [dot(top, u_ref[2 * p + e, :HALF, :]), dot(bottom, u_ref[2 * p + e])], axis=0
            )
            qt_ref[p, :, e * LANES : (e + 1) * LANES] = jnp.where(
                lane < HD, qf - pu[:, :LANES], is_one - pu[:, LANES:]
            ).astype(BF16)
            if e == 0:
                total = pltpu.roll(pu[:, :LANES], HD, 1)
            else:
                py_ref[p] = jnp.where(lane < HD, total, pu[:, :LANES])

    def to_group(slot, e, peer):
        return pltpu.make_async_remote_copy(
            src_ref=send1.at[slot, e],
            dst_ref=recv1.at[place],
            send_sem=send_sem1.at[slot, e],
            recv_sem=recv_sem1.at[place],
            device_id=(base + peer, head),
            device_id_type=MESH,
        )

    copies = []
    for load in (loads[5], loads[0], loads[1]):
        load.wait()
    for load in loads[2:5]:
        load.start()
    steps = (2, 1, 3, 0)
    for batch in ((0, 1), (2, 3)):
        pairs = [lax.rem(chip + steps[slot], PAIRS) for slot in batch]
        build_maps(batch, pairs)
        if batch[0] == 0:
            pl.semaphore_wait(barrier, GROUP - 1 + GROUPS - 1 + 2)
        for slot, p in zip(batch, pairs):
            if steps[slot]:
                for e in (0, 1):
                    copy = to_group(slot, e, 2 * p + e)
                    copy.start()
                    copies.append(copy)
            else:
                copy = to_group(slot, 1 - core, 2 * p + 1 - core)
                copy.start()
                copies.append(copy)
                recv1[place] = send1[slot, core]

    loads[2].wait()
    build_outputs(0)
    build_outputs(1)

    pad = jnp.zeros((LANES - FEAT, 2 * LANES), BF16)
    for j in range(GROUP):
        @pl.when(place != j)
        def _(j=j):
            pltpu.make_async_remote_copy(
                src_ref=send1.at[0, 0],
                dst_ref=recv1.at[j],
                send_sem=send_sem1.at[0, 0],
                recv_sem=recv_sem1.at[j],
                device_id=(base + j, head),
                device_id_type=MESH,
            ).wait_recv()

    def as_left(step_map):
        return jnp.where(lane_f < HD, step_map[:, :LANES], step_map[:, LANES:]).astype(BF16)

    def then(earlier, left, later):
        padded = jnp.concatenate([earlier.astype(BF16), pad], axis=0)
        return earlier + later + dot(left, padded)

    lefts, maps = zip(*[unpack(recv1[j]) for j in range(GROUP)])
    m01, m23, m45, m67 = [then(maps[j], lefts[j + 1], maps[j + 1]) for j in (0, 2, 4, 6)]
    m03 = then(m01, as_left(m23), m23)
    m47 = then(m45, as_left(m67), m67)
    m07 = then(m03, as_left(m47), m47)
    send2[...] = pack(m07[:, :LANES], m07[:, LANES:])

    def to_groups(step):
        return pltpu.make_async_remote_copy(
            src_ref=send2,
            dst_ref=recv2.at[group],
            send_sem=send_sem2.at[step - 1],
            recv_sem=recv_sem2.at[group],
            device_id=((group + step) * GROUP + place, head),
            device_id_type=MESH,
        )

    for step in range(1, GROUPS):
        @pl.when(group + step < GROUPS)
        def _(step=step):
            to_groups(step).start()

    m02 = then(m01, lefts[2], maps[2])
    m04 = then(m03, lefts[4], maps[4])
    m05 = then(m03, as_left(m45), m45)
    m46 = then(m45, lefts[6], maps[6])
    m06 = then(m03, as_left(m46), m46)
    for j, step_map in enumerate((maps[0], m01, m02, m03, m04, m05, m06)):
        prefix[j] = step_map.astype(BF16)
    build_outputs(2)

    loads[3].wait()
    first = jnp.concatenate([start_ref[...], jnp.zeros((HD, LANES - HD - 1), F32)], axis=1)
    entry = jnp.transpose(jnp.concatenate([jnp.zeros((HD, LANES), F32), first], axis=0))[:FEAT]
    for g in range(GROUPS - 1):
        @pl.when(g < group)
        def _(g=g):
            pltpu.make_async_remote_copy(
                src_ref=send2,
                dst_ref=recv2.at[g],
                send_sem=send_sem2.at[0],
                recv_sem=recv_sem2.at[g],
                device_id=(g * GROUP + place, head),
                device_id_type=MESH,
            ).wait_recv()

    half_pad = jnp.zeros((LANES - FEAT, LANES), BF16)

    def apply(left, step_map, old):
        padded = jnp.concatenate([old.astype(BF16), half_pad], axis=0)
        return old + jnp.where(lane_f < HD, 0.0, step_map) + dot(left, padded)

    passed = [
        unpack(jnp.where(g < group, recv2[g].astype(F32), 0.0)) for g in range(GROUPS - 1)
    ]
    for left, step_map in passed:
        entry = apply(left, step_map[:, :LANES], entry)

    def pack_state(rows):
        return jnp.concatenate(
            [
                jnp.where(lane[:32] < HD, pltpu.roll(rows[:32], HD, 1), rows[32:HD]),
                rows[HD:],
            ],
            axis=0,
        ).astype(BF16)

    send3[0] = pack_state(entry)
    for j in range(1, GROUP):
        before = prefix[j - 1].astype(F32)
        send3[j] = pack_state(apply(as_left(before), before[:, :LANES], entry))

    def back(step):
        peer = lax.rem(place + step, GROUP)
        return pltpu.make_async_remote_copy(
            src_ref=send3.at[peer],
            dst_ref=recv3.at[place],
            send_sem=send_sem3.at[step - 1],
            recv_sem=recv_sem3.at[place],
            device_id=(base + peer, head),
            device_id_type=MESH,
        )

    for step in (4, 5, 3, 2, 6, 7, 1):
        copy = back(step)
        copy.start()
        copies.append(copy)
    recv3[place] = send3[place]

    build_outputs(3)

    for step in range(1, GROUP):
        source = lax.rem(place + step, GROUP)
        pltpu.make_async_remote_copy(
            src_ref=send3.at[0],
            dst_ref=recv3.at[source],
            send_sem=send_sem3.at[0],
            recv_sem=recv_sem3.at[source],
            device_id=(base + source, head),
            device_id_type=MESH,
        ).wait_recv()
    loads[4].wait()

    def unpack_state(h):
        wide = recv3[h].astype(F32)
        turned = pltpu.roll(wide, HD, 1)
        odd = h % 2
        ours = (lane[: PACKED] < HD) != (odd == 1)
        same = jnp.where(ours, wide, 0.0)
        other = jnp.where(ours, turned, 0.0)
        if odd:
            parts = [other[:32], same[:32], same[32:]]
        else:
            parts = [same[:32], other[:32], other[32:]]
        return jnp.concatenate([jnp.concatenate(parts, axis=0).astype(BF16), rest], axis=0)

    states = [
        jnp.concatenate([unpack_state(2 * p), unpack_state(2 * p + 1)], axis=0)
        for p in range(PAIRS)
    ]

    def outputs_of(block):
        rows = pl.ds(pl.multiple_of(block * ROWS, ROWS), ROWS)
        return jnp.concatenate(
            [
                (dot(qt_ref[p, rows, :], states[p]) + py_ref[p, rows, :]).astype(BF16)
                for p in range(PAIRS)
            ],
            axis=1,
        )

    half = WIDTH // 2

    def project(z, side, piece):
        at = side * half + piece * 512
        return dot(z, w_ref[:, at : at + 512])

    def send(source, target, send_at, recv_at, peer):
        copy = pltpu.make_async_remote_copy(
            src_ref=source, dst_ref=target, send_sem=send_at, recv_sem=recv_at,
            device_id=(seq, peer), device_id_type=MESH,
        )
        copy.start()
        return copy

    def arrived(target, recv_at, peer):
        pltpu.make_async_remote_copy(
            src_ref=target, dst_ref=target, send_sem=far_send_sem.at[0, 0], recv_sem=recv_at,
            device_id=(seq, peer), device_id_type=MESH,
        ).wait_recv()

    chunks = range(CHUNKS)

    def chunk_rows(chunk):
        return pl.ds(chunk * CHUNK, CHUNK)

    z = outputs_of(lax.rem(head + 2, RING))
    for side, peer in ((0, up), (1, down)):
        for piece in (0, 1):
            far_send[side, :, piece * 512 : (piece + 1) * 512] = project(z, side, piece).astype(BF16)
        for chunk in chunks:
            copies.append(
                send(
                    far_send.at[side, chunk_rows(chunk)], far_recv.at[side, chunk_rows(chunk)],
                    far_send_sem.at[side, chunk], far_recv_sem.at[side, chunk], peer,
                )
            )
    z_near = [outputs_of(up), outputs_of(down)]
    def send_near(way, side, peer):
        copies.append(
            send(
                near_send.at[way, side], near_recv.at[way, side],
                near_send_sem.at[way], near_recv_sem.at[way], peer,
            )
        )

    for way in (0, 1):
        side = 1 - way
        for piece in (0, 1):
            near_send[way, side, :, piece * 512 : (piece + 1) * 512] = project(
                z_near[way], side, piece
            ).astype(BF16)
        send_near(way, side, (up, down)[way])
    merged = [[project(z_near[way], way, piece) for piece in (0, 1)] for way in (0, 1)]
    for chunk in chunks:
        for way, peer, source in ((0, up, down), (1, down, up)):
            rows = chunk_rows(chunk)
            arrived(far_recv.at[way, rows], far_recv_sem.at[way, chunk], source)
            for piece in (0, 1):
                cols = slice(piece * 512, (piece + 1) * 512)
                near_send[way, way, rows, cols] = (
                    merged[way][piece][chunk * CHUNK : (chunk + 1) * CHUNK]
                    + far_recv[way, rows, cols].astype(F32)
                ).astype(BF16)
            copies.append(
                send(
                    near_send.at[way, way, rows], near_recv.at[way, way, rows],
                    merge_send_sem.at[way, chunk], merge_recv_sem.at[way, chunk], peer,
                )
            )
    z = outputs_of(head)
    own = [[project(z, side, piece) for piece in (0, 1)] for side in (0, 1)]
    sources = (down, up)
    for way in (0, 1):
        arrived(near_recv.at[way, 1 - way], near_recv_sem.at[way], sources[way])
    for chunk in chunks:
        for way in (0, 1):
            arrived(
                near_recv.at[way, way, chunk_rows(chunk)], merge_recv_sem.at[way, chunk], sources[way]
            )
    for side in (0, 1):
        for piece in (0, 1):
            cols = slice(piece * 512, (piece + 1) * 512)
            at = side * half + piece * 512
            out_ref[:, at : at + 512] = (
                own[side][piece]
                + near_recv[0, side, :, cols].astype(F32)
                + near_recv[1, side, :, cols].astype(F32)
            ).astype(BF16)

    for copy in copies:
        copy.wait_send()
    for step in range(1, GROUPS):
        @pl.when(group + step < GROUPS)
        def _(step=step):
            to_groups(step).wait_send()


def per_device(queries, keys, values, rates, start_state, out_weight):
    hbm = pl.BlockSpec(memory_space=pl.ANY)
    vmem = pl.BlockSpec(memory_space=pltpu.VMEM)
    dma = pltpu.SemaphoreType.DMA
    half = WIDTH // 2
    return pl.pallas_call(
        kernel,
        out_shape=jax.ShapeDtypeStruct((ROWS, WIDTH), BF16),
        in_specs=[hbm] * 6,
        out_specs=vmem,
        scratch_shapes=[
            pltpu.VMEM((TOK, 8 * HD), BF16),
            pltpu.VMEM((TOK, 8 * HD), BF16),
            pltpu.VMEM((TOK, 8 * HD), BF16),
            pltpu.VMEM((8 * HD, WIDTH), BF16),
            pltpu.VMEM((HD, HD + 1), F32),
            pltpu.VMEM((2 * PAIRS, TOK), F32),
            pltpu.VMEM((2 * PAIRS, TOK, 2 * LANES), BF16),
            pltpu.VMEM((2 * PAIRS, LANES, TOK), BF16),
            pltpu.VMEM((PAIRS, TOK, 2 * LANES), BF16),
            pltpu.VMEM((PAIRS, TOK, LANES), F32),
            pltpu.VMEM((PAIRS, 2, FEAT, LANES), BF16),
            pltpu.VMEM((GROUP, FEAT, LANES), BF16),
            pltpu.VMEM((GROUP - 1, FEAT, 2 * LANES), BF16),
            pltpu.VMEM((FEAT, LANES), BF16),
            pltpu.VMEM((GROUPS, FEAT, LANES), BF16),
            pltpu.VMEM((GROUP, PACKED, LANES), BF16),
            pltpu.VMEM((GROUP, PACKED, LANES), BF16),
            pltpu.VMEM((2, ROWS, half), BF16),
            pltpu.VMEM((2, ROWS, half), BF16),
            pltpu.VMEM((2, 2, ROWS, half), BF16),
            pltpu.VMEM((2, 2, ROWS, half), BF16),
            dma((6,)),
            dma((PAIRS, 2)),
            dma((GROUP,)),
            dma((GROUPS - 1,)),
            dma((GROUPS,)),
            dma((GROUP - 1,)),
            dma((GROUP,)),
            dma((2, CHUNKS)),
            dma((2, CHUNKS)),
            dma((2,)),
            dma((2,)),
            dma((2, CHUNKS)),
            dma((2, CHUNKS)),
        ],
        compiler_params=pltpu.CompilerParams(
            collective_id=0, has_side_effects=True, vmem_limit_bytes=60 * 1024 * 1024
        ),
    )(queries, keys, values, jnp.transpose(rates), start_state, out_weight)


def solution(mesh):
    in_specs = (
        P("seq", "head"),
        P("seq", "head"),
        P("seq", "head"),
        P("seq", "head"),
        P("head", None, None),
        P("head", None),
    )
    out_specs = P(("seq", "head"), None)
    return jax.shard_map(
        per_device, mesh=mesh, in_specs=in_specs, out_specs=out_specs, check_vma=False
    )
```

time: 40.7 us -> 34.7 us (0.85)
  local copies, waits for them, and re-layouts: 6.79 us -> 1.67 us
  Pallas kernels: 33.6 us -> 32.9 us
    unnamed x13 -> x1, local copies, waits for them, and re-layouts: 6.79 us -> 1.67 us
    pallas_call x1, Pallas kernels: 33.6 us -> 32.9 us  [per_device(): pl.pallas_call(kernel, out_shape=jax.ShapeDtypeStruct((ROWS, WIDTH), BF16...]
where the time goes in v1:
time: 34.7 us; the launch traced here: 34.6 us
  Pallas kernels  32.9 us (95%)
  local copies, waits for them, and re-layouts  1.67 us (5%)
    pallas_call x1, Pallas kernels, per_device(): pl.pallas_call(kernel, out_shape=jax.ShapeDtypeStruct((ROWS, WIDTH), BF16...  32.9 us
    unnamed x1, local copies, waits for them, and re-layouts  1.67 us

profile of v1, /device:TPU:6, one launch (start us, length us, event | category | flops | bytes accessed | tf_op | source)
XLA Modules:
  0.0 34.6 jit_solution(1315240137810215512)
XLA Ops:
  0.0 32.9 %shard_map.64 = bf16[64,2048]{1,0:T(8,128)(2,1)} custom-call(bf16[256,512]{1,0:T(8,128)(2,1)} %q_hbm.1, bf16[256,512]{1,0:T(8,128)(2,1)} %k_hbm.1, bf16[256,512]{1,0:T(8,128)(2,1)} %v_hbm.1, f32[8,256]{1,0:T(8,128)} %bitcast.1, f32[8,64,65]{2,1,0:T(8,128)} %start_hbm.1, bf16[512,2048]{1,0:T(8,128)(2,1)} %w_hbm.1), custom_call_target="tpu_custom_call" | custom-call | tf_op jit(solution)/shard_map/pallas_call | solution.py:473
  32.9 1.7 %copy.8 = bf16[64,2048]{1,0:T(8,128)(2,1)} copy(bf16[64,2048]{1,0:T(8,128)(2,1)} %shard_map.64) | data formatting | bytes 524288

commit v2 on v1

--- a/solution.py
+++ b/solution.py
@@ -442,20 +442,21 @@
     sources = (down, up)
     for way in (0, 1):
         arrived(near_recv.at[way, 1 - way], near_recv_sem.at[way], sources[way])
-    for chunk in chunks:
-        for way in (0, 1):
-            arrived(
-                near_recv.at[way, way, chunk_rows(chunk)], merge_recv_sem.at[way, chunk], sources[way]
-            )
     for side in (0, 1):
         for piece in (0, 1):
-            cols = slice(piece * 512, (piece + 1) * 512)
-            at = side * half + piece * 512
-            out_ref[:, at : at + 512] = (
-                own[side][piece]
-                + near_recv[0, side, :, cols].astype(F32)
-                + near_recv[1, side, :, cols].astype(F32)
-            ).astype(BF16)
+            own[side][piece] = own[side][piece] + near_recv[
+                1 - side, side, :, piece * 512 : (piece + 1) * 512
+            ].astype(F32)
+    for chunk in chunks:
+        rows = chunk_rows(chunk)
+        for side in (0, 1):
+            arrived(near_recv.at[side, side, rows], merge_recv_sem.at[side, chunk], sources[side])
+            for piece in (0, 1):
+                at = side * half + piece * 512
+                out_ref[rows, at : at + 512] = (
+                    own[side][piece][chunk * CHUNK : (chunk + 1) * CHUNK]
+                    + near_recv[side, side, rows, piece * 512 : (piece + 1) * 512].astype(F32)
+                ).astype(BF16)
 
     for copy in copies:
         copy.wait_send()
@@ -512,7 +513,7 @@
             dma((2, CHUNKS)),
         ],
         compiler_params=pltpu.CompilerParams(
-            collective_id=0, has_side_effects=True, vmem_limit_bytes=60 * 1024 * 1024
+            collective_id=0, has_side_effects=True, vmem_limit_bytes=54784 * 1024
         ),
     )(queries, keys, values, jnp.transpose(rates), start_state, out_weight)
 

time: 34.7 us -> 33.3 us (0.960)
  Pallas kernels: 32.9 us -> 31.7 us
    pallas_call x1, Pallas kernels: 32.9 us -> 31.7 us  [per_device(): pl.pallas_call(kernel, out_shape=jax.ShapeDtypeStruct((ROWS, WIDTH), BF16...]
    unnamed x1 -> x3, local copies, waits for them, and re-layouts: 1.67 us -> 1.4 us
where the time goes in v2:
time: 33.3 us; the launch traced here: 33.1 us
  Pallas kernels  31.7 us (95%)
  local copies, waits for them, and re-layouts  1.4 us (4%)
    pallas_call x1, Pallas kernels, per_device(): pl.pallas_call(kernel, out_shape=jax.ShapeDtypeStruct((ROWS, WIDTH), BF16...  31.7 us
    unnamed x3, local copies, waits for them, and re-layouts  1.4 us

profile of v2, /device:TPU:6, one launch (start us, length us, event | category | flops | bytes accessed | tf_op | source)
XLA Modules:
  0.0 33.1 jit_solution(8377929854117854900)
XLA Ops:
  0.0 0.0 copy-start
  0.0 0.7 %copy-done = f32[256,8]{0,1:T(8,128)S(1)} copy-done((f32[256,8]{0,1:T(8,128)S(1)}, f32[256,8]{0,1:T(8,128)}, u32[]{:S(2)}) %copy-start) | copy-done | bytes 8216
  0.7 31.7 %shard_map.64 = bf16[64,2048]{1,0:T(8,128)(2,1)S(1)} custom-call(bf16[256,512]{1,0:T(8,128)(2,1)} %q_hbm.1, bf16[256,512]{1,0:T(8,128)(2,1)} %k_hbm.1, bf16[256,512]{1,0:T(8,128)(2,1)} %v_hbm.1, f32[8,256]{1,0:T(8,128)S(1)} %bitcast.1, f32[8,64,65]{2,1,0:T(8,128)} %start_hbm.1, bf16[512,2048]{1,0:T(8,128)(2,1)} %w_hbm.1), custom_call_target="tpu_custom_call" | custom-call | tf_op jit(solution)/shard_map/pallas_call | solution.py:474
  32.4 0.7 %copy.8 = bf16[64,2048]{1,0:T(8,128)(2,1)} copy(bf16[64,2048]{1,0:T(8,128)(2,1)S(1)} %shard_map.64) | data formatting | bytes 524288
Async XLA Ops:
  0.0 0.7 %copy-start = (f32[256,8]{0,1:T(8,128)S(1)}, f32[256,8]{0,1:T(8,128)}, u32[]{:S(2)}) copy-start(f32[256,8]{0,1:T(8,128)} %param.9) | copy-start | bytes 24580

commit v3 on v2

--- a/solution.py
+++ b/solution.py
@@ -18,7 +18,7 @@
 PACKED = 48
 WIDTH = 2048
 ROWS = TOK // RING
-CHUNKS = 4
+CHUNKS = 1
 CHUNK = ROWS // CHUNKS
 MESH = pl.DeviceIdType.MESH
 F32 = jnp.float32
@@ -195,7 +195,7 @@
         load.wait()
     for load in loads[2:5]:
         load.start()
-    steps = (2, 1, 3, 0)
+    steps = (2, 3, 1, 0)
     for batch in ((0, 1), (2, 3)):
         pairs = [lax.rem(chip + steps[slot], PAIRS) for slot in batch]
         build_maps(batch, pairs)

time: 33.3 us -> 32.3 us (0.970)
  Pallas kernels: 31.7 us -> 30.7 us
    pallas_call x1, Pallas kernels: 31.7 us -> 30.7 us  [per_device(): pl.pallas_call(kernel, out_shape=jax.ShapeDtypeStruct((ROWS, WIDTH), BF16...]
where the time goes in v3:
time: 32.3 us; the launch traced here: 32.1 us
  Pallas kernels  30.7 us (95%)
  local copies, waits for them, and re-layouts  1.4 us (4%)
    pallas_call x1, Pallas kernels, per_device(): pl.pallas_call(kernel, out_shape=jax.ShapeDtypeStruct((ROWS, WIDTH), BF16...  30.7 us
    unnamed x3, local copies, waits for them, and re-layouts  1.4 us

profile of v3, /device:TPU:6, one launch (start us, length us, event | category | flops | bytes accessed | tf_op | source)
XLA Modules:
  0.0 32.1 jit_solution(13157861914918402025)
XLA Ops:
  0.0 0.0 copy-start
  0.0 0.7 %copy-done = f32[256,8]{0,1:T(8,128)S(1)} copy-done((f32[256,8]{0,1:T(8,128)S(1)}, f32[256,8]{0,1:T(8,128)}, u32[]{:S(2)}) %copy-start) | copy-done | bytes 8216
  0.7 30.7 %shard_map.64 = bf16[64,2048]{1,0:T(8,128)(2,1)S(1)} custom-call(bf16[256,512]{1,0:T(8,128)(2,1)} %q_hbm.1, bf16[256,512]{1,0:T(8,128)(2,1)} %k_hbm.1, bf16[256,512]{1,0:T(8,128)(2,1)} %v_hbm.1, f32[8,256]{1,0:T(8,128)S(1)} %bitcast.1, f32[8,64,65]{2,1,0:T(8,128)} %start_hbm.1, bf16[512,2048]{1,0:T(8,128)(2,1)} %w_hbm.1), custom_call_target="tpu_custom_call" | custom-call | tf_op jit(solution)/shard_map/pallas_call | solution.py:474
  31.4 0.7 %copy.8 = bf16[64,2048]{1,0:T(8,128)(2,1)} copy(bf16[64,2048]{1,0:T(8,128)(2,1)S(1)} %shard_map.64) | data formatting | bytes 524288
Async XLA Ops:
  0.0 0.7 %copy-start = (f32[256,8]{0,1:T(8,128)S(1)}, f32[256,8]{0,1:T(8,128)}, u32[]{:S(2)}) copy-start(f32[256,8]{0,1:T(8,128)} %param.9) | copy-start | bytes 24580

commit v4 on v3

--- a/solution.py
+++ b/solution.py
@@ -254,7 +254,7 @@
             device_id_type=MESH,
         )
 
-    for step in range(1, GROUPS):
+    for step in (3, 2, 1):
         @pl.when(group + step < GROUPS)
         def _(step=step):
             to_groups(step).start()

time: 32.3 us -> 32.3 us (level)
  no operation moved by 1% of the time
where the time goes in v4:
time: 32.3 us; the launch traced here: 32.1 us
  Pallas kernels  30.7 us (95%)
  local copies, waits for them, and re-layouts  1.4 us (4%)
    pallas_call x1, Pallas kernels, per_device(): pl.pallas_call(kernel, out_shape=jax.ShapeDtypeStruct((ROWS, WIDTH), BF16...  30.7 us
    unnamed x3, local copies, waits for them, and re-layouts  1.4 us

profile of v4, /device:TPU:6, one launch (start us, length us, event | category | flops | bytes accessed | tf_op | source)
XLA Modules:
  0.0 32.1 jit_solution(18315378475074331066)
XLA Ops:
  0.0 0.0 copy-start
  0.0 0.7 %copy-done = f32[256,8]{0,1:T(8,128)S(1)} copy-done((f32[256,8]{0,1:T(8,128)S(1)}, f32[256,8]{0,1:T(8,128)}, u32[]{:S(2)}) %copy-start) | copy-done | bytes 8216
  0.7 30.7 %shard_map.64 = bf16[64,2048]{1,0:T(8,128)(2,1)S(1)} custom-call(bf16[256,512]{1,0:T(8,128)(2,1)} %q_hbm.1, bf16[256,512]{1,0:T(8,128)(2,1)} %k_hbm.1, bf16[256,512]{1,0:T(8,128)(2,1)} %v_hbm.1, f32[8,256]{1,0:T(8,128)S(1)} %bitcast.1, f32[8,64,65]{2,1,0:T(8,128)} %start_hbm.1, bf16[512,2048]{1,0:T(8,128)(2,1)} %w_hbm.1), custom_call_target="tpu_custom_call" | custom-call | tf_op jit(solution)/shard_map/pallas_call | solution.py:474
  31.4 0.7 %copy.8 = bf16[64,2048]{1,0:T(8,128)(2,1)} copy(bf16[64,2048]{1,0:T(8,128)(2,1)S(1)} %shard_map.64) | data formatting | bytes 524288
Async XLA Ops:
  0.0 0.7 %copy-start = (f32[256,8]{0,1:T(8,128)S(1)}, f32[256,8]{0,1:T(8,128)}, u32[]{:S(2)}) copy-start(f32[256,8]{0,1:T(8,128)} %param.9) | copy-start | bytes 24580
